TPU v7x, 32 devices: a whole 2x2x4 slice. The times are simulated.
32 devices in a mesh: groups: 2 (over y), age: 4 (over z), span: 2 (over x), blade: 2 (over core).
Axes of the slice: x: 2, y: 2, z: 4, core: 2. Of those that a mesh axis runs over, the one named last changes fastest.
Arguments:
- surface_mu: float32 [32, 4, 64, 128], P(('groups', 'age'), 'blade', None, 'span'), parts along dimension 0, may hold values from -6 to 6
- centroid_body: float32 [3, 4, 64, 128], P(None, 'blade', None, 'span'), may hold values from -0.04 to 1.01
- area_normal: float32 [3, 4, 64, 128], P(None, 'blade', None, 'span'), may hold values from -0.12 to 0.12
- te_body: float32 [3, 4, 128], P(None, 'blade', 'span'), may hold values from -0.04 to 1.01
- wake_state: float32 [4, 4, 64, 2, 128], P(None, 'blade', ('groups', 'age'), 'span'), parts along dimension 2, may hold values from -2 to 2
- pairs: int32 [4, 64, 2, 8], P('blade', ('groups', 'age'), 'span'), parts along dimension 1, may hold values from -1 to 71, as said below
- az_index: int32 [6], P('groups'), parts along dimension 0, may hold values from 0 to 15
- free_stream: float32 [6], P('groups'), parts along dimension 0, may hold values from -3 to 3
Outputs:
- wake_final: float32 [4, 4, 64, 2, 128], P(None, 'blade', ('groups', 'age'), 'span'), parts along dimension 2
- wake_velocity: float32 [3, 4, 64, 2, 128], P(None, 'blade', ('groups', 'age'), 'span'), parts along dimension 2
There are 2 independent parts, one for each index of `groups`. A program takes and returns all parts, laid end to end along the dimension named above; an argument that names none is the same for every part. Nothing has to cross between parts.
Inputs may be any that keep to these rules, and one draw needn't show every extreme that they name: Rows come in age blocks of 16 rows (8 tiles), spanwise panels in strips of 64. An entry v >= 0 of pairs[b, t, s, :] names tile v % 8 of age block t // 8 + v // 24 - 1 in strip s + (v // 8) % 3 - 1 of the same blade; -1 marks an empty slot. In each aligned block of 2 blades, one age block and one strip, at most 64 entries are not -1, and exactly 64 in one such block.
All inputs are finite; a program needn't handle non-finite values.
Results may differ from a plain program's by a relative error of at most 0.0003.
Values sent between devices are 32-bit elements; how exact they have to be, the bound alone decides.
A program may use at most 64 MiB of HBM per device.

v0:
```python
import math
import jax
import jax.numpy as jnp
from jax import lax
from jax.sharding import PartitionSpec as P

CB = 8
time_step = 0.05
near_core = 0.0025
far_core = 0.01
inv_four_pi = 0.25 / math.pi


def spread(shard, axis, root):
    mine = lax.axis_index(axis) == root
    return lax.psum(jnp.where(mine, shard, jnp.zeros_like(shard)), axis)


def with_halo(cells, sides, width):
    for axis, dim in sides:
        count = lax.axis_size(axis)
        ends = count - 1
        head = lax.slice_in_dim(cells, 0, width, axis=dim)
        tail = lax.slice_in_dim(cells, cells.shape[dim] - width, cells.shape[dim], axis=dim)
        cells = jnp.concatenate(
            [
                lax.ppermute(tail, axis, [(i, (i + 1) % count) for i in range(ends)]),
                cells,
                lax.ppermute(head, axis, [((i + 1) % count, i) for i in range(ends)]),
            ],
            axis=dim,
        )
    return cells


def shifted(value, axis, steps):
    count = lax.axis_size(axis)
    first, last = (max(0, -steps), min(count, count - steps))
    return lax.ppermute(value, axis, [(source, source + steps) for source in range(first, last)])


def rotate(vector, cosine, sine_val):
    return jnp.stack(
        [
            vector[0] * cosine - vector[1] * sine_val,
            vector[0] * sine_val + vector[1] * cosine,
            vector[2],
        ]
    )


def coarse_sum(values, block_size):
    shape = values.shape
    grouped = values.reshape(
        shape[:-2] + (shape[-2] // block_size, block_size, shape[-1] // block_size, block_size)
    )
    return jnp.sum(grouped, axis=(-3, -1))


def far_velocity(targets, centers, moments):
    separation = targets[:, :, None] - centers[:, None, :]
    dist_sq = jnp.sum(separation * separation, axis=0) + far_core
    inverse = 1.0 / jnp.sqrt(dist_sq)
    inverse_cube = inverse * inverse * inverse
    projection = jnp.sum(moments[:, None, :] * separation, axis=0)
    values = (
        3.0 * projection * inverse_cube * inverse * inverse * separation
        - moments[:, None, :] * inverse_cube
    )
    return inv_four_pi * jnp.sum(values, axis=2)


def near_velocity(targets, sources, strengths):
    separation = targets[:, :, None] - sources[:, None, :]
    dist_sq = jnp.sum(separation * separation, axis=0) + near_core
    weight = 1.0 / (dist_sq * jnp.sqrt(dist_sq))
    cross_prod = jnp.stack(
        [
            strengths[1][None, :] * separation[2] - strengths[2][None, :] * separation[1],
            strengths[2][None, :] * separation[0] - strengths[0][None, :] * separation[2],
            strengths[0][None, :] * separation[1] - strengths[1][None, :] * separation[0],
        ]
    )
    return inv_four_pi * jnp.sum(cross_prod * weight[None], axis=2)


def sheet_strength(pos_pad, mu_pad):
    pos_r = 0.5 * (pos_pad[:, :, 2:, 1:-1] - pos_pad[:, :, :-2, 1:-1])
    pos_s = 0.5 * (pos_pad[:, :, 1:-1, 2:] - pos_pad[:, :, 1:-1, :-2])
    mu_r = 0.5 * (mu_pad[:, 2:, 1:-1] - mu_pad[:, :-2, 1:-1])
    mu_s = 0.5 * (mu_pad[:, 1:-1, 2:] - mu_pad[:, 1:-1, :-2])
    return mu_s[None] * pos_r - mu_r[None] * pos_s


def grouped_map(kernel, operands):
    length = jax.tree.leaves(operands)[0].shape[0]
    turn_count = math.gcd(length, 16)
    shaped = jax.tree.map(
        lambda array: array.reshape((turn_count, length // turn_count) + array.shape[1:]), operands
    )
    result = lax.map(jax.vmap(kernel), shaped)
    return result.reshape((length,) + result.shape[2:])


def far_kernel(centers, moments):

    def apply_one(target_tile):
        return far_velocity(target_tile, centers, moments)

    return apply_one


def near_kernel(bundle):
    return near_velocity(bundle[0], bundle[1], bundle[2])


def on_device(
    surface_mu, centroid_body, area_normal, te_body, wake_state, pairs, az_index, free_stream
):
    az_dev, blade_group, chord_len, span_dev = surface_mu.shape
    tile_dev = wake_state.shape[2]
    lanes = wake_state.shape[4]
    rows_dev = tile_dev * lanes // span_dev
    slot_tile = pairs.shape[3]
    step_count = az_index.shape[0]
    age_count = lax.axis_size("age")
    span_count = lax.axis_size("span")
    blade_count = lax.axis_size("blade")
    age_pos = lax.axis_index("age")
    span_pos = lax.axis_index("span")
    blade_pos = lax.axis_index("blade")
    naz_total = az_dev * age_count
    blade_total = blade_group * blade_count
    tile_local = blade_group * tile_dev
    block_cells = chord_len // CB * (span_dev // CB)
    per_device = blade_group * block_cells
    column = jnp.arange(per_device * span_count * blade_count, dtype=jnp.int32)
    column_blade = (
        column // per_device % blade_count * blade_group + column % per_device // block_cells
    )
    column_frac = column_blade.astype(jnp.float32) / blade_total
    local_frac = (blade_pos * blade_group + jnp.arange(blade_group, dtype=jnp.int32)).astype(
        jnp.float32
    ) / blade_total
    center_local = (coarse_sum(centroid_body, CB) / (CB * CB)).reshape(3, per_device)
    center_all = lax.all_gather(center_local, ("span", "blade"), axis=1, tiled=True)
    sheet_grid = wake_state[:, :, :, 0, :].reshape(4, blade_group, rows_dev, span_dev)
    velocity = jnp.zeros((3, blade_group, tile_dev, lanes), jnp.float32)
    for step_num in range(step_count):
        azimuth = az_index[step_num]
        mu_now = lax.dynamic_index_in_dim(surface_mu, azimuth % az_dev, 0, keepdims=False)
        moment_local = coarse_sum(mu_now[None] * area_normal, CB).reshape(3, per_device)
        trailing_local = (mu_now[:, chord_len - 1, :] - mu_now[:, 0, :]).reshape(
            blade_group * span_dev
        )
        moment_local, trailing_local = (moment_local, trailing_local)
        moment_got, trailing = (
            spread(moment_local, "age", azimuth // az_dev),
            spread(trailing_local, "age", azimuth // az_dev),
        )
        moment_all = lax.all_gather(moment_got, ("span", "blade"), axis=1, tiled=True)
        turn_frac = azimuth.astype(jnp.float32) / naz_total
        source_angle = 2.0 * math.pi * (turn_frac + column_frac)
        source_cos = jnp.cos(source_angle)
        source_sin = jnp.sin(source_angle)
        centers = rotate(center_all, source_cos, source_sin)
        moments = rotate(moment_all, source_cos, source_sin)
        padded = with_halo(sheet_grid, (("age", 2), ("span", 3)), 1)
        pos_pad = padded[:3]
        top_rows = jnp.where(age_pos == 0, pos_pad[:, :, 1, :], pos_pad[:, :, 0, :])
        bottom_rows = jnp.where(
            age_pos == age_count - 1, pos_pad[:, :, -2, :], pos_pad[:, :, -1, :]
        )
        pos_pad = jnp.concatenate(
            [top_rows[:, :, None], pos_pad[:, :, 1:-1], bottom_rows[:, :, None]], 2
        )
        left_cols = jnp.where(span_pos == 0, pos_pad[..., 1], pos_pad[..., 0])
        right_cols = jnp.where(span_pos == span_count - 1, pos_pad[..., -2], pos_pad[..., -1])
        pos_pad = jnp.concatenate(
            [left_cols[..., None], pos_pad[..., 1:-1], right_cols[..., None]], 3
        )
        strength = sheet_strength(pos_pad, padded[3])
        pos_tiles = sheet_grid[:3].reshape(3, blade_group, tile_dev, lanes)
        str_tiles = strength.reshape(3, blade_group, tile_dev, lanes)
        targets = pos_tiles.reshape(3, tile_local, lanes).transpose(1, 0, 2)
        far_field = grouped_map(far_kernel(centers, moments), targets)
        blocks = jnp.concatenate([pos_tiles, str_tiles], 0).transpose(1, 2, 0, 3)[:, None, None]
        beside_all = with_halo(blocks, (("age", 1), ("span", 2)), 1)
        source_table = beside_all.reshape(blade_group, 9 * tile_dev, 6, lanes)
        pair_ids = pairs[:, :, 0, :]
        live_mask = pair_ids >= 0
        safe_ids = jnp.maximum(pair_ids, 0)
        picked = source_table[jnp.arange(blade_group, dtype=jnp.int32)[:, None, None], safe_ids]
        weights = live_mask.astype(jnp.float32)[:, :, :, None, None]
        sources = (
            picked[:, :, :, :3]
            .reshape(tile_local, slot_tile, 3, lanes)
            .transpose(0, 2, 1, 3)
            .reshape(tile_local, 3, slot_tile * lanes)
        )
        strengths = (
            (picked[:, :, :, 3:] * weights)
            .reshape(tile_local, slot_tile, 3, lanes)
            .transpose(0, 2, 1, 3)
            .reshape(tile_local, 3, slot_tile * lanes)
        )
        near_flat = grouped_map(near_kernel, (targets, sources, strengths))
        far_part = far_field.transpose(1, 0, 2).reshape(3, blade_group, tile_dev, lanes)
        near_part = near_flat.transpose(1, 0, 2).reshape(3, blade_group, tile_dev, lanes)
        velocity = free_stream[:, None, None, None] + far_part + near_part
        moved_pos = sheet_grid[:3] + time_step * velocity.reshape(
            3, blade_group, rows_dev, span_dev
        )
        moved_state = jnp.concatenate([moved_pos, sheet_grid[3:4]], 0)
        incoming = shifted(moved_state[:, :, -1, :], "age", 1)
        blade_angle = 2.0 * math.pi * (turn_frac + local_frac)
        te_pos = rotate(te_body, jnp.cos(blade_angle)[:, None], jnp.sin(blade_angle)[:, None])
        shed_row = jnp.concatenate([te_pos, trailing.reshape(1, blade_group, span_dev)], 0)
        incoming = jnp.where(age_pos == 0, shed_row, incoming)
        sheet_grid = jnp.concatenate([incoming[:, :, None, :], moved_state[:, :, :-1, :]], 2)
    final_tiles = sheet_grid.reshape(4, blade_group, tile_dev, lanes)
    return (final_tiles[:, :, :, None, :], velocity[:, :, :, None, :])


def solution(mesh):
    in_specs = (
        P(("groups", "age"), "blade", None, "span"),
        P(None, "blade", None, "span"),
        P(None, "blade", None, "span"),
        P(None, "blade", "span"),
        P(None, "blade", ("groups", "age"), "span", None),
        P("blade", ("groups", "age"), "span", None),
        P("groups"),
        P("groups"),
    )
    out_specs = (
        P(None, "blade", ("groups", "age"), "span", None),
        P(None, "blade", ("groups", "age"), "span", None),
    )
    return jax.shard_map(
        on_device, mesh=mesh, in_specs=in_specs, out_specs=out_specs, check_vma=False
    )
```

profile of v0, /device:TPU:0, one launch (start us, length us, event | category | flops | bytes accessed | tf_op | source)
XLA Modules:
  0.0 256.7 jit_solution(8771473071030211586)
XLA Ops:
  2.7 4.9 %collective-permute-start = (f32[4,2,1,64]{3,1,2,0:T(2,128)S(1)}, f32[4,2,1,64]{3,1,2,0:T(2,128)S(1)}, u32[]{:S(2)}, u32[]{:S(2)}) collective-permute-start(f32[4,2,1,64]{3,1,2,0:T(2,128)S(1)} %copy.303), channel_id=1, source_target_pairs={{0,4},{4,8},{8,12},{1,5},{5,9},{9,13},{2,6},{6,10},{10,14},{3,7},{... | collective-permute-start | bytes 6152 | tf_op jit(solution)/shard_map/ppermute | solution.py:27
  26.2 13.3 %all-reduce = (f32[3,128]{1,0:T(4,128)S(1)}, f32[1,2,64]{2,1,0:T(2,128)S(1)}, f32[3,128]{1,0:T(4,128)S(1)}, f32[1,2,64]{2,1,0:T(2,128)S(1)}, f32[3,128]{1,0:T(4,128)S(1)}, /*index=5*/f32[1,2,64]{2,1,0:T(2,128)S(1)}) all-reduce(f32[3,128]{1,0:T(4,128)S(1)} %select_n.377, ...), channel_id=1, replica_groups=mesh['groups'=2,'age'=4,'span'=2,'blade'=2] {'age'}, use_global_device_ids=true, to_apply=%region_5.6 | all-reduce | flops 1536 | bytes 12288 | tf_op jit(solution)/shard_map/psum | solution.py:16
  39.6 5.2 %all_gather.12 = f32[3,512]{1,0:T(4,128)S(1)} all-gather(f32[3,128]{1,0:T(4,128)S(1)} %get-tuple-element.344), channel_id=1, replica_groups=mesh['groups'=2,'age'=4,'span'=2,'blade'=2] {'span','blade'}, dimensions={1}, use_global_device_ids=true | all-gather | bytes 7680 | tf_op jit(solution)/shard_map/all_gather | solution.py:161
  45.5 5.2 %all_gather.13 = f32[3,512]{1,0:T(4,128)S(1)} all-gather(f32[3,128]{1,0:T(4,128)S(1)} %div.142), channel_id=1, replica_groups=mesh['groups'=2,'age'=4,'span'=2,'blade'=2] {'span','blade'}, dimensions={1}, use_global_device_ids=true | all-gather | bytes 7680 | tf_op jit(solution)/shard_map/all_gather | solution.py:146
  51.0 9.9 %while.60 = (s32[]{:T(128)}, f32[16,1,3,128]{3,2,1,0:T(4,128)S(1)}, f32[3,512]{1,0:T(4,128)S(1)}, f32[16,1,3,128]{3,2,1,0:T(4,128)S(1)}, f32[3,512]{1,0:T(4,128)S(1)}, /*index=5*/s32[]{:T(128)}) while((s32[]{:T(128)}, f32[16,1,3,128]{3,2,1,0:T(4,128)S(1)}, f32[3,512]{1,0:T(4,128)S(1)}, f32[16,1,3,128]{3,2,1,0:T(4,128)S(1)}, ...), condition=%wide.region_10.11_spmd, body=%wide.region_6.10_spmd.sunk | while | flops 2293762 | bytes 2133589 | solution.py:101
  60.9 5.2 %all_gather.14 = f32[3,512]{1,0:T(4,128)S(1)} all-gather(f32[3,128]{1,0:T(4,128)S(1)} %get-tuple-element.346), channel_id=1, replica_groups=mesh['groups'=2,'age'=4,'span'=2,'blade'=2] {'span','blade'}, dimensions={1}, use_global_device_ids=true | all-gather | bytes 7680 | tf_op jit(solution)/shard_map/all_gather | solution.py:161
  68.5 4.5 %collective-permute-start.2 = (f32[4,2,18,1]{3,1,2,0:T(2,128)S(1)}, f32[4,2,18,1]{3,1,2,0:T(2,128)S(1)}, u32[]{:S(2)}, u32[]{:S(2)}) collective-permute-start(f32[4,2,18,1]{3,1,2,0:T(2,128)S(1)} %get-tuple-element.398), channel_id=1, source_target_pairs={{0,2},{1,3},{4,6},{5,7},{8,10},{9,11},{12,14},{13,15},{16,18},{17,... | collective-permute-start | bytes 1736 | tf_op jit(solution)/shard_map/ppermute | solution.py:27
  77.7 4.5 %collective-permute-start.4 = (f32[2,1,1,8,6,128]{5,3,0,4,2,1:T(8,128)S(1)}, f32[2,1,1,8,6,128]{5,3,0,4,2,1:T(8,128)S(1)}, u32[]{:S(2)}, u32[]{:S(2)}) collective-permute-start(f32[2,1,1,8,6,128]{5,3,0,4,2,1:T(8,128)S(1)} %maximum_bitcast_fusion.3), channel_id=1, source_target_pairs={{0,4},{4,8},{8,12},{1,5},{5,9},{9,13},{2,6},{6,10},{10,14},{3,7},{... | collective-permute-start | bytes 147464 | tf_op jit(solution)/shard_map/ppermute | solution.py:27
  85.3 4.6 %collective-permute-start.6 = (f32[2,3,1,8,6,128]{5,3,0,4,2,1:T(8,128)S(1)}, f32[2,3,1,8,6,128]{5,3,0,4,2,1:T(8,128)S(1)}, u32[]{:S(2)}, u32[]{:S(2)}) collective-permute-start(f32[2,3,1,8,6,128]{5,3,0,4,2,1:T(8,128)S(1)} %pad_maximum_fusion.3), channel_id=1, source_target_pairs={{0,2},{1,3},{4,6},{5,7},{8,10},{9,11},{12,14},{13,15},{16,18},{17,... | collective-permute-start | bytes 442376 | tf_op jit(solution)/shard_map/ppermute | solution.py:27
  94.0 19.9 %while.61 = (s32[]{:T(128)}, f32[16,1,3,128]{3,2,1,0:T(4,128)S(1)}, f32[16,1,3,1024]{3,0,2,1:T(8,128)S(1)}, f32[16,1,3,128]{3,2,1,0:T(4,128)S(1)}, f32[16,1,3,1024]{3,0,2,1:T(8,128)S(1)}, /*index=5*/s32[]{:T(128)}) while((s32[]{:T(128)}, f32[16,1,3,128]{3,2,1,0:T(4,128)S(1)}, f32[16,1,3,1024]{3,0,2,1:T(8,128)S(1)}, ...), condition=%wide.region_14.15_spmd, body=%wide.region_11.14_spmd.sunk | while | flops 4587522 | bytes 8560217 | solution.py:101
  114.2 4.2 %collective-permute-start.8 = (f32[4,2,64]{2,1,0:T(2,128)S(1)}, f32[4,2,64]{2,1,0:T(2,128)S(1)}, u32[]{:S(2)}, u32[]{:S(2)}) collective-permute-start(f32[4,2,64]{2,1,0:T(2,128)S(1)} %get-tuple-element.403), channel_id=1, source_target_pairs={{0,4},{4,8},{8,12},{1,5},{5,9},{9,13},{2,6},{6,10},{10,14},{3,7},{... | collective-permute-start | bytes 6152 | tf_op jit(solution)/shard_map/ppermute | solution.py:39
  127.5 4.5 %collective-permute-start.11 = (f32[4,2,18,1]{3,1,0,2:T(2,128)S(1)}, f32[4,2,18,1]{3,1,0,2:T(2,128)S(1)}, u32[]{:S(2)}, u32[]{:S(2)}) collective-permute-start(f32[4,2,18,1]{3,1,0,2:T(2,128)S(1)} %get-tuple-element.396), channel_id=1, source_target_pairs={{0,2},{1,3},{4,6},{5,7},{8,10},{9,11},{12,14},{13,15},{16,18},{17,... | collective-permute-start | bytes 1736 | tf_op jit(solution)/shard_map/ppermute | solution.py:27
  136.7 4.5 %collective-permute-start.13 = (f32[2,1,1,8,6,128]{5,3,0,4,2,1:T(8,128)S(1)}, f32[2,1,1,8,6,128]{5,3,0,4,2,1:T(8,128)S(1)}, u32[]{:S(2)}, u32[]{:S(2)}) collective-permute-start(f32[2,1,1,8,6,128]{5,3,0,4,2,1:T(8,128)S(1)} %maximum_bitcast_fusion.4), channel_id=1, source_target_pairs={{0,4},{4,8},{8,12},{1,5},{5,9},{9,13},{2,6},{6,10},{10,14},{3,7},{... | collective-permute-start | bytes 147464 | tf_op jit(solution)/shard_map/ppermute | solution.py:27
  141.3 5.5 %all_gather.15 = f32[3,512]{1,0:T(4,128)S(1)} all-gather(f32[3,128]{1,0:T(4,128)S(1)} %get-tuple-element.348), channel_id=1, replica_groups=mesh['groups'=2,'age'=4,'span'=2,'blade'=2] {'span','blade'}, dimensions={1}, use_global_device_ids=true | all-gather | bytes 7680 | tf_op jit(solution)/shard_map/all_gather | solution.py:161
  148.3 4.7 %collective-permute-start.15 = (f32[2,3,1,8,6,128]{5,3,0,4,2,1:T(8,128)S(1)}, f32[2,3,1,8,6,128]{5,3,0,4,2,1:T(8,128)S(1)}, u32[]{:S(2)}, u32[]{:S(2)}) collective-permute-start(f32[2,3,1,8,6,128]{5,3,0,4,2,1:T(8,128)S(1)} %pad_maximum_fusion.4), channel_id=1, source_target_pairs={{0,2},{1,3},{4,6},{5,7},{8,10},{9,11},{12,14},{13,15},{16,18},{17,... | collective-permute-start | bytes 442376 | tf_op jit(solution)/shard_map/ppermute | solution.py:27
  153.1 9.9 %while.62 = (s32[]{:T(128)}, f32[16,1,3,128]{3,2,1,0:T(4,128)S(1)}, f32[3,512]{1,0:T(4,128)S(1)}, f32[16,1,3,128]{3,2,1,0:T(4,128)S(1)}, f32[3,512]{1,0:T(4,128)S(1)}, /*index=5*/s32[]{:T(128)}) while((s32[]{:T(128)}, f32[16,1,3,128]{3,2,1,0:T(4,128)S(1)}, f32[3,512]{1,0:T(4,128)S(1)}, f32[16,1,3,128]{3,2,1,0:T(4,128)S(1)}, ...), condition=%wide.region_21.22_spmd, body=%wide.region_17.21_spmd.sunk | while | flops 2293762 | bytes 2133589 | solution.py:101
  164.6 19.9 %while.63 = (s32[]{:T(128)}, f32[16,1,3,128]{3,2,1,0:T(4,128)S(1)}, f32[16,1,3,1024]{3,0,2,1:T(8,128)S(1)}, f32[16,1,3,128]{3,2,1,0:T(4,128)S(1)}, f32[16,1,3,1024]{3,0,2,1:T(8,128)S(1)}, /*index=5*/s32[]{:T(128)}) while((s32[]{:T(128)}, f32[16,1,3,128]{3,2,1,0:T(4,128)S(1)}, f32[16,1,3,1024]{3,0,2,1:T(8,128)S(1)}, ...), condition=%wide.region_25.26_spmd, body=%wide.region_22.25_spmd.sunk | while | flops 4587522 | bytes 8560217 | solution.py:101
  191.6 4.2 %collective-permute-done.19 = f32[4,2,1,64]{3,1,2,0:T(2,128)S(1)} collective-permute-done((f32[4,2,1,64]{3,1,2,0:T(2,128)S(1)}, f32[4,2,1,64]{3,1,2,0:T(2,128)S(1)}, u32[]{:S(2)}, u32[]{:S(2)}) %collective-permute-start.19) | collective-permute-done | bytes 2080 | tf_op jit(solution)/shard_map/ppermute | solution.py:29
  197.3 4.5 %collective-permute-start.20 = (f32[4,2,18,1]{3,1,2,0:T(2,128)S(1)}, f32[4,2,18,1]{3,1,2,0:T(2,128)S(1)}, u32[]{:S(2)}, u32[]{:S(2)}) collective-permute-start(f32[4,2,18,1]{3,1,2,0:T(2,128)S(1)} %get-tuple-element.394), channel_id=1, source_target_pairs={{0,2},{1,3},{4,6},{5,7},{8,10},{9,11},{12,14},{13,15},{16,18},{17,... | collective-permute-start | bytes 1736 | tf_op jit(solution)/shard_map/ppermute | solution.py:27
  206.6 4.5 %collective-permute-start.22 = (f32[2,1,1,8,6,128]{5,3,0,4,2,1:T(8,128)S(1)}, f32[2,1,1,8,6,128]{5,3,0,4,2,1:T(8,128)S(1)}, u32[]{:S(2)}, u32[]{:S(2)}) collective-permute-start(f32[2,1,1,8,6,128]{5,3,0,4,2,1:T(8,128)S(1)} %maximum_bitcast_fusion.5), channel_id=1, source_target_pairs={{0,4},{4,8},{8,12},{1,5},{5,9},{9,13},{2,6},{6,10},{10,14},{3,7},{... | collective-permute-start | bytes 147464 | tf_op jit(solution)/shard_map/ppermute | solution.py:27
  214.2 4.6 %collective-permute-start.24 = (f32[2,3,1,8,6,128]{5,3,0,4,2,1:T(8,128)S(1)}, f32[2,3,1,8,6,128]{5,3,0,4,2,1:T(8,128)S(1)}, u32[]{:S(2)}, u32[]{:S(2)}) collective-permute-start(f32[2,3,1,8,6,128]{5,3,0,4,2,1:T(8,128)S(1)} %pad_maximum_fusion.5), channel_id=1, source_target_pairs={{0,2},{1,3},{4,6},{5,7},{8,10},{9,11},{12,14},{13,15},{16,18},{17,... | collective-permute-start | bytes 442376 | tf_op jit(solution)/shard_map/ppermute | solution.py:27
  218.8 9.9 %while.64 = (s32[]{:T(128)}, f32[16,1,3,128]{3,2,1,0:T(4,128)S(1)}, f32[3,512]{1,0:T(4,128)S(1)}, f32[16,1,3,128]{3,2,1,0:T(4,128)S(1)}, f32[3,512]{1,0:T(4,128)S(1)}, /*index=5*/s32[]{:T(128)}) while((s32[]{:T(128)}, f32[16,1,3,128]{3,2,1,0:T(4,128)S(1)}, f32[3,512]{1,0:T(4,128)S(1)}, f32[16,1,3,128]{3,2,1,0:T(4,128)S(1)}, ...), condition=%wide.region_32.33_spmd, body=%wide.region_28.32_spmd.sunk | while | flops 2293762 | bytes 2133589 | solution.py:101
  230.3 19.9 %while.65 = (s32[]{:T(128)}, f32[16,1,3,128]{3,2,1,0:T(4,128)S(1)}, f32[16,1,3,1024]{3,0,2,1:T(8,128)S(1)}, f32[16,1,3,128]{3,2,1,0:T(4,128)S(1)}, f32[16,1,3,1024]{3,0,2,1:T(8,128)S(1)}, /*index=5*/s32[]{:T(128)}) while((s32[]{:T(128)}, f32[16,1,3,128]{3,2,1,0:T(4,128)S(1)}, f32[16,1,3,1024]{3,0,2,1:T(8,128)S(1)}, ...), condition=%wide.region_36.37_spmd, body=%wide.region_33.36_spmd.sunk | while | flops 4587522 | bytes 8560217 | solution.py:101
  250.4 4.2 %collective-permute-start.26 = (f32[4,2,64]{2,1,0:T(2,128)S(1)}, f32[4,2,64]{2,1,0:T(2,128)S(1)}, u32[]{:S(2)}, u32[]{:S(2)}) collective-permute-start(f32[4,2,64]{2,1,0:T(2,128)S(1)} %bitcast.385), channel_id=1, source_target_pairs={{0,4},{4,8},{8,12},{1,5},{5,9},{9,13},{2,6},{6,10},{10,14},{3,7},{... | collective-permute-start | bytes 6152 | tf_op jit(solution)/shard_map/ppermute | solution.py:39
  (981 shorter events, 146.4 us)
Async XLA Ops:
  2.7 64.2 %collective-permute-start = (f32[4,2,1,64]{3,1,2,0:T(2,128)S(1)}, f32[4,2,1,64]{3,1,2,0:T(2,128)S(1)}, u32[]{:S(2)}, u32[]{:S(2)}) collective-permute-start(f32[4,2,1,64]{3,1,2,0:T(2,128)S(1)} %copy.303), channel_id=1, source_target_pairs={{0,4},{4,8},{8,12},{1,5},{5,9},{9,13},{2,6},{6,10},{10,14},{3,7},{... | collective-permute-start | bytes 6152 | tf_op jit(solution)/shard_map/ppermute | solution.py:27
  7.7 59.3 %collective-permute-start.1 = (f32[4,2,1,64]{3,1,2,0:T(2,128)S(1)}, f32[4,2,1,64]{3,1,2,0:T(2,128)S(1)}, u32[]{:S(2)}, u32[]{:S(2)}) collective-permute-start(f32[4,2,1,64]{3,1,2,0:T(2,128)S(1)} %copy.304), channel_id=1, source_target_pairs={{4,0},{8,4},{12,8},{5,1},{9,5},{13,9},{6,2},{10,6},{14,10},{7,3},{... | collective-permute-start | bytes 6152 | tf_op jit(solution)/shard_map/ppermute | solution.py:29
  67.2 6.4 %collective-permute-start.3 = (f32[4,2,18,1]{3,1,2,0:T(2,128)S(1)}, f32[4,2,18,1]{3,1,2,0:T(2,128)S(1)}, u32[]{:S(2)}, u32[]{:S(2)}) collective-permute-start(f32[4,2,18,1]{3,1,2,0:T(2,128)S(1)} %get-tuple-element.399), channel_id=1, source_target_pairs={{2,0},{3,1},{6,4},{7,5},{10,8},{11,9},{14,12},{15,13},{18,16},{19,... | collective-permute-start | bytes 1736 | tf_op jit(solution)/shard_map/ppermute | solution.py:29
  68.5 6.5 %collective-permute-start.2 = (f32[4,2,18,1]{3,1,2,0:T(2,128)S(1)}, f32[4,2,18,1]{3,1,2,0:T(2,128)S(1)}, u32[]{:S(2)}, u32[]{:S(2)}) collective-permute-start(f32[4,2,18,1]{3,1,2,0:T(2,128)S(1)} %get-tuple-element.398), channel_id=1, source_target_pairs={{0,2},{1,3},{4,6},{5,7},{8,10},{9,11},{12,14},{13,15},{16,18},{17,... | collective-permute-start | bytes 1736 | tf_op jit(solution)/shard_map/ppermute | solution.py:27
  76.4 6.0 %collective-permute-start.5 = (f32[2,1,1,8,6,128]{5,3,0,4,2,1:T(8,128)S(1)}, f32[2,1,1,8,6,128]{5,3,0,4,2,1:T(8,128)S(1)}, u32[]{:S(2)}, u32[]{:S(2)}) collective-permute-start(f32[2,1,1,8,6,128]{5,3,0,4,2,1:T(8,128)S(1)} %maximum_bitcast_fusion.3), channel_id=1, source_target_pairs={{4,0},{8,4},{12,8},{5,1},{9,5},{13,9},{6,2},{10,6},{14,10},{7,3},{... | collective-permute-start | bytes 147464 | tf_op jit(solution)/shard_map/ppermute | solution.py:29
  77.7 6.3 %collective-permute-start.4 = (f32[2,1,1,8,6,128]{5,3,0,4,2,1:T(8,128)S(1)}, f32[2,1,1,8,6,128]{5,3,0,4,2,1:T(8,128)S(1)}, u32[]{:S(2)}, u32[]{:S(2)}) collective-permute-start(f32[2,1,1,8,6,128]{5,3,0,4,2,1:T(8,128)S(1)} %maximum_bitcast_fusion.3), channel_id=1, source_target_pairs={{0,4},{4,8},{8,12},{1,5},{5,9},{9,13},{2,6},{6,10},{10,14},{3,7},{... | collective-permute-start | bytes 147464 | tf_op jit(solution)/shard_map/ppermute | solution.py:27
  84.0 7.0 %collective-permute-start.7 = (f32[2,3,1,8,6,128]{5,3,0,4,2,1:T(8,128)S(1)}, f32[2,3,1,8,6,128]{5,3,0,4,2,1:T(8,128)S(1)}, u32[]{:S(2)}, u32[]{:S(2)}) collective-permute-start(f32[2,3,1,8,6,128]{5,3,0,4,2,1:T(8,128)S(1)} %pad_maximum_fusion.3), channel_id=1, source_target_pairs={{2,0},{3,1},{6,4},{7,5},{10,8},{11,9},{14,12},{15,13},{18,16},{19,... | collective-permute-start | bytes 442376 | tf_op jit(solution)/shard_map/ppermute | solution.py:29
  85.3 7.2 %collective-permute-start.6 = (f32[2,3,1,8,6,128]{5,3,0,4,2,1:T(8,128)S(1)}, f32[2,3,1,8,6,128]{5,3,0,4,2,1:T(8,128)S(1)}, u32[]{:S(2)}, u32[]{:S(2)}) collective-permute-start(f32[2,3,1,8,6,128]{5,3,0,4,2,1:T(8,128)S(1)} %pad_maximum_fusion.3), channel_id=1, source_target_pairs={{0,2},{1,3},{4,6},{5,7},{8,10},{9,11},{12,14},{13,15},{16,18},{17,... | collective-permute-start | bytes 442376 | tf_op jit(solution)/shard_map/ppermute | solution.py:27
  114.2 6.3 %collective-permute-start.8 = (f32[4,2,64]{2,1,0:T(2,128)S(1)}, f32[4,2,64]{2,1,0:T(2,128)S(1)}, u32[]{:S(2)}, u32[]{:S(2)}) collective-permute-start(f32[4,2,64]{2,1,0:T(2,128)S(1)} %get-tuple-element.403), channel_id=1, source_target_pairs={{0,4},{4,8},{8,12},{1,5},{5,9},{9,13},{2,6},{6,10},{10,14},{3,7},{... | collective-permute-start | bytes 6152 | tf_op jit(solution)/shard_map/ppermute | solution.py:39
  120.5 5.5 %collective-permute-start.10 = (f32[4,2,1,64]{3,1,0,2:T(2,128)S(1)}, f32[4,2,1,64]{3,1,0,2:T(2,128)S(1)}, u32[]{:S(2)}, u32[]{:S(2)}) collective-permute-start(f32[4,2,1,64]{3,1,0,2:T(2,128)S(1)} %fusion.57), channel_id=1, source_target_pairs={{4,0},{8,4},{12,8},{5,1},{9,5},{13,9},{6,2},{10,6},{14,10},{7,3},{... | collective-permute-start | bytes 6152 | tf_op jit(solution)/shard_map/ppermute | solution.py:29
  126.2 6.2 %collective-permute-start.12 = (f32[4,2,18,1]{3,1,0,2:T(2,128)S(1)}, f32[4,2,18,1]{3,1,0,2:T(2,128)S(1)}, u32[]{:S(2)}, u32[]{:S(2)}) collective-permute-start(f32[4,2,18,1]{3,1,0,2:T(2,128)S(1)} %get-tuple-element.397), channel_id=1, source_target_pairs={{2,0},{3,1},{6,4},{7,5},{10,8},{11,9},{14,12},{15,13},{18,16},{19,... | collective-permute-start | bytes 1736 | tf_op jit(solution)/shard_map/ppermute | solution.py:29
  127.5 6.5 %collective-permute-start.11 = (f32[4,2,18,1]{3,1,0,2:T(2,128)S(1)}, f32[4,2,18,1]{3,1,0,2:T(2,128)S(1)}, u32[]{:S(2)}, u32[]{:S(2)}) collective-permute-start(f32[4,2,18,1]{3,1,0,2:T(2,128)S(1)} %get-tuple-element.396), channel_id=1, source_target_pairs={{0,2},{1,3},{4,6},{5,7},{8,10},{9,11},{12,14},{13,15},{16,18},{17,... | collective-permute-start | bytes 1736 | tf_op jit(solution)/shard_map/ppermute | solution.py:27
  135.4 11.5 %collective-permute-start.14 = (f32[2,1,1,8,6,128]{5,3,0,4,2,1:T(8,128)S(1)}, f32[2,1,1,8,6,128]{5,3,0,4,2,1:T(8,128)S(1)}, u32[]{:S(2)}, u32[]{:S(2)}) collective-permute-start(f32[2,1,1,8,6,128]{5,3,0,4,2,1:T(8,128)S(1)} %maximum_bitcast_fusion.4), channel_id=1, source_target_pairs={{4,0},{8,4},{12,8},{5,1},{9,5},{13,9},{6,2},{10,6},{14,10},{7,3},{... | collective-permute-start | bytes 147464 | tf_op jit(solution)/shard_map/ppermute | solution.py:29
  136.7 10.2 %collective-permute-start.13 = (f32[2,1,1,8,6,128]{5,3,0,4,2,1:T(8,128)S(1)}, f32[2,1,1,8,6,128]{5,3,0,4,2,1:T(8,128)S(1)}, u32[]{:S(2)}, u32[]{:S(2)}) collective-permute-start(f32[2,1,1,8,6,128]{5,3,0,4,2,1:T(8,128)S(1)} %maximum_bitcast_fusion.4), channel_id=1, source_target_pairs={{0,4},{4,8},{8,12},{1,5},{5,9},{9,13},{2,6},{6,10},{10,14},{3,7},{... | collective-permute-start | bytes 147464 | tf_op jit(solution)/shard_map/ppermute | solution.py:27
  147.0 16.1 %collective-permute-start.16 = (f32[2,3,1,8,6,128]{5,3,0,4,2,1:T(8,128)S(1)}, f32[2,3,1,8,6,128]{5,3,0,4,2,1:T(8,128)S(1)}, u32[]{:S(2)}, u32[]{:S(2)}) collective-permute-start(f32[2,3,1,8,6,128]{5,3,0,4,2,1:T(8,128)S(1)} %pad_maximum_fusion.4), channel_id=1, source_target_pairs={{2,0},{3,1},{6,4},{7,5},{10,8},{11,9},{14,12},{15,13},{18,16},{19,... | collective-permute-start | bytes 442376 | tf_op jit(solution)/shard_map/ppermute | solution.py:29
  148.3 14.8 %collective-permute-start.15 = (f32[2,3,1,8,6,128]{5,3,0,4,2,1:T(8,128)S(1)}, f32[2,3,1,8,6,128]{5,3,0,4,2,1:T(8,128)S(1)}, u32[]{:S(2)}, u32[]{:S(2)}) collective-permute-start(f32[2,3,1,8,6,128]{5,3,0,4,2,1:T(8,128)S(1)} %pad_maximum_fusion.4), channel_id=1, source_target_pairs={{0,2},{1,3},{4,6},{5,7},{8,10},{9,11},{12,14},{13,15},{16,18},{17,... | collective-permute-start | bytes 442376 | tf_op jit(solution)/shard_map/ppermute | solution.py:27
  184.8 5.5 %collective-permute-start.17 = (f32[4,2,64]{2,1,0:T(2,128)S(1)}, f32[4,2,64]{2,1,0:T(2,128)S(1)}, u32[]{:S(2)}, u32[]{:S(2)}) collective-permute-start(f32[4,2,64]{2,1,0:T(2,128)S(1)} %get-tuple-element.401), channel_id=1, source_target_pairs={{0,4},{4,8},{8,12},{1,5},{5,9},{9,13},{2,6},{6,10},{10,14},{3,7},{... | collective-permute-start | bytes 6152 | tf_op jit(solution)/shard_map/ppermute | solution.py:39
  196.0 6.2 %collective-permute-start.21 = (f32[4,2,18,1]{3,1,2,0:T(2,128)S(1)}, f32[4,2,18,1]{3,1,2,0:T(2,128)S(1)}, u32[]{:S(2)}, u32[]{:S(2)}) collective-permute-start(f32[4,2,18,1]{3,1,2,0:T(2,128)S(1)} %get-tuple-element.395), channel_id=1, source_target_pairs={{2,0},{3,1},{6,4},{7,5},{10,8},{11,9},{14,12},{15,13},{18,16},{19,... | collective-permute-start | bytes 1736 | tf_op jit(solution)/shard_map/ppermute | solution.py:29
  197.3 6.5 %collective-permute-start.20 = (f32[4,2,18,1]{3,1,2,0:T(2,128)S(1)}, f32[4,2,18,1]{3,1,2,0:T(2,128)S(1)}, u32[]{:S(2)}, u32[]{:S(2)}) collective-permute-start(f32[4,2,18,1]{3,1,2,0:T(2,128)S(1)} %get-tuple-element.394), channel_id=1, source_target_pairs={{0,2},{1,3},{4,6},{5,7},{8,10},{9,11},{12,14},{13,15},{16,18},{17,... | collective-permute-start | bytes 1736 | tf_op jit(solution)/shard_map/ppermute | solution.py:27
  205.3 6.0 %collective-permute-start.23 = (f32[2,1,1,8,6,128]{5,3,0,4,2,1:T(8,128)S(1)}, f32[2,1,1,8,6,128]{5,3,0,4,2,1:T(8,128)S(1)}, u32[]{:S(2)}, u32[]{:S(2)}) collective-permute-start(f32[2,1,1,8,6,128]{5,3,0,4,2,1:T(8,128)S(1)} %maximum_bitcast_fusion.5), channel_id=1, source_target_pairs={{4,0},{8,4},{12,8},{5,1},{9,5},{13,9},{6,2},{10,6},{14,10},{7,3},{... | collective-permute-start | bytes 147464 | tf_op jit(solution)/shard_map/ppermute | solution.py:29
  206.6 6.3 %collective-permute-start.22 = (f32[2,1,1,8,6,128]{5,3,0,4,2,1:T(8,128)S(1)}, f32[2,1,1,8,6,128]{5,3,0,4,2,1:T(8,128)S(1)}, u32[]{:S(2)}, u32[]{:S(2)}) collective-permute-start(f32[2,1,1,8,6,128]{5,3,0,4,2,1:T(8,128)S(1)} %maximum_bitcast_fusion.5), channel_id=1, source_target_pairs={{0,4},{4,8},{8,12},{1,5},{5,9},{9,13},{2,6},{6,10},{10,14},{3,7},{... | collective-permute-start | bytes 147464 | tf_op jit(solution)/shard_map/ppermute | solution.py:27
  212.9 15.9 %collective-permute-start.25 = (f32[2,3,1,8,6,128]{5,3,0,4,2,1:T(8,128)S(1)}, f32[2,3,1,8,6,128]{5,3,0,4,2,1:T(8,128)S(1)}, u32[]{:S(2)}, u32[]{:S(2)}) collective-permute-start(f32[2,3,1,8,6,128]{5,3,0,4,2,1:T(8,128)S(1)} %pad_maximum_fusion.5), channel_id=1, source_target_pairs={{2,0},{3,1},{6,4},{7,5},{10,8},{11,9},{14,12},{15,13},{18,16},{19,... | collective-permute-start | bytes 442376 | tf_op jit(solution)/shard_map/ppermute | solution.py:29
  214.2 14.6 %collective-permute-start.24 = (f32[2,3,1,8,6,128]{5,3,0,4,2,1:T(8,128)S(1)}, f32[2,3,1,8,6,128]{5,3,0,4,2,1:T(8,128)S(1)}, u32[]{:S(2)}, u32[]{:S(2)}) collective-permute-start(f32[2,3,1,8,6,128]{5,3,0,4,2,1:T(8,128)S(1)} %pad_maximum_fusion.5), channel_id=1, source_target_pairs={{0,2},{1,3},{4,6},{5,7},{8,10},{9,11},{12,14},{13,15},{16,18},{17,... | collective-permute-start | bytes 442376 | tf_op jit(solution)/shard_map/ppermute | solution.py:27
  250.4 5.6 %collective-permute-start.26 = (f32[4,2,64]{2,1,0:T(2,128)S(1)}, f32[4,2,64]{2,1,0:T(2,128)S(1)}, u32[]{:S(2)}, u32[]{:S(2)}) collective-permute-start(f32[4,2,64]{2,1,0:T(2,128)S(1)} %bitcast.385), channel_id=1, source_target_pairs={{0,4},{4,8},{8,12},{1,5},{5,9},{9,13},{2,6},{6,10},{10,14},{3,7},{... | collective-permute-start | bytes 6152 | tf_op jit(solution)/shard_map/ppermute | solution.py:39
  (6 other events, 75.8 us)
where the time goes:
time: 258 us; the launch traced here: 257 us
  other arithmetic  91.1 us (35%)
  starting transfers between devices  77.3 us (30%)
  blocking collectives  34.4 us (13%)
  waiting for transfers between devices  20.1 us (8%)
  local copies, waits for them, and re-layouts  16.5 us (6%)
  between operations  11.3 us (4%)
  loops' own time  5.87 us (2%)
    ppermute x12, starting transfers between devices, with_halo(): lax.ppermute(tail, axis, [(i, (i + 1) % count) for i in range(ends)])  49.9 us
    all_gather x3, blocking collectives, on_device(): lax.all_gather(moment_got, ('span', 'blade'), axis=1, tiled=True)  15.9 us
    ppermute x12, starting transfers between devices, with_halo(): lax.ppermute(head, axis, [((i + 1) % count, i) for i in range(ends)])  15.5 us
    sub x48, other arithmetic, near_velocity(): strengths[1][None, :] * separation[2]  14.4 us
    reduce_sum x48, other arithmetic, far_velocity(): return inv_four_pi * jnp.sum(values, axis=2)  13.4 us
    psum x1, blocking collectives, spread(): return lax.psum(jnp.where(mine, shard, jnp.zeros_like(shard)), axis)  13.3 us
    ppermute x3, starting transfers between devices, shifted(): lax.ppermute(value, axis, [(source, source + steps) for source in range(f...  11.9 us
    reduce_sum x48, other arithmetic, near_velocity(): dist_sq = jnp.sum(separation * separation, axis=0) + near_core  10.6 us
  transfers between devices with their start and end apart: 27, of which 14 were waited for; matrix products, arithmetic and copies ran while one was open for 15% of the time, Pallas kernels for 0%

commit v1 on v0

--- a/solution.py
+++ b/solution.py
@@ -13,7 +13,7 @@
 
 def spread(shard, axis, root):
     mine = lax.axis_index(axis) == root
-    return lax.psum(jnp.where(mine, shard, jnp.zeros_like(shard)), axis)
+    return jnp.sum(lax.all_gather(jnp.where(mine, shard, jnp.zeros_like(shard)), axis), axis=0)
 
 
 def with_halo(cells, sides, width):

time: 258 us -> 303 us (1.17)
  blocking collectives: 34.4 us -> 82.7 us
  starting transfers between devices: 77.3 us -> 56.7 us
  waiting for transfers between devices: 20.1 us -> 38.1 us
    all_gather x0 -> x6, blocking collectives: none -> 62.1 us  [spread(): lax.all_gather(jnp.where(mine, shard, jnp.zeros_like(shard)), axis)]
    ppermute x12, waiting for transfers between devices: 10.2 us -> 34.2 us  [with_halo(): lax.ppermute(head, axis, [((i + 1) % count, i) for i in range(ends)])]
    ppermute x12, starting transfers between devices: 49.9 us -> 32 us  [with_halo(): lax.ppermute(tail, axis, [(i, (i + 1) % count) for i in range(ends)])]
    psum x1 -> x0, blocking collectives: 13.3 us -> none  [spread(): return lax.psum(jnp.where(mine, shard, jnp.zeros_like(shard)), axis)]
    ppermute x12, waiting for transfers between devices: 9.29 us -> 3.32 us  [with_halo(): lax.ppermute(tail, axis, [(i, (i + 1) % count) for i in range(ends)])]
  transfers between devices with their start and end apart: 27 -> 27, of which waited for: 14 -> 15; matrix products, arithmetic and copies ran while one was open for 15% -> 13% of each run, Pallas kernels for 0% -> 0%
where the time goes in v1:
time: 303 us; the launch traced here: 302 us
  other arithmetic  91.2 us (30%)
  blocking collectives  82.7 us (27%)
  starting transfers between devices  56.7 us (19%)
  waiting for transfers between devices  38.1 us (13%)
  local copies, waits for them, and re-layouts  15.6 us (5%)
  between operations  11.5 us (4%)
  loops' own time  5.87 us (2%)
    all_gather x6, blocking collectives, spread(): lax.all_gather(jnp.where(mine, shard, jnp.zeros_like(shard)), axis)  62.1 us
    ppermute x12, waiting for transfers between devices, with_halo(): lax.ppermute(head, axis, [((i + 1) % count, i) for i in range(ends)])  34.2 us
    ppermute x12, starting transfers between devices, with_halo(): lax.ppermute(tail, axis, [(i, (i + 1) % count) for i in range(ends)])  32 us
    ppermute x12, starting transfers between devices, with_halo(): lax.ppermute(head, axis, [((i + 1) % count, i) for i in range(ends)])  15.7 us
    all_gather x3, blocking collectives, on_device(): lax.all_gather(moment_got, ('span', 'blade'), axis=1, tiled=True)  15.5 us
    sub x48, other arithmetic, near_velocity(): strengths[1][None, :] * separation[2]  14.4 us
    reduce_sum x48, other arithmetic, far_velocity(): return inv_four_pi * jnp.sum(values, axis=2)  13.4 us
    reduce_sum x48, other arithmetic, near_velocity(): dist_sq = jnp.sum(separation * separation, axis=0) + near_core  10.6 us
  transfers between devices with their start and end apart: 27, of which 15 were waited for; matrix products, arithmetic and copies ran while one was open for 13% of the time, Pallas kernels for 0%

profile of v1, /device:TPU:0, one launch (start us, length us, event | category | flops | bytes accessed | tf_op | source)
XLA Modules:
  0.0 301.7 jit_solution(8546588677814079648)
XLA Ops:
  2.7 4.9 %collective-permute-start = (f32[4,2,1,64]{3,1,2,0:T(2,128)S(1)}, f32[4,2,1,64]{3,1,2,0:T(2,128)S(1)}, u32[]{:S(2)}, u32[]{:S(2)}) collective-permute-start(f32[4,2,1,64]{3,1,2,0:T(2,128)S(1)} %copy.362), channel_id=1, source_target_pairs={{0,4},{4,8},{8,12},{1,5},{5,9},{9,13},{2,6},{6,10},{10,14},{3,7},{... | collective-permute-start | bytes 6152 | tf_op jit(solution)/shard_map/ppermute | solution.py:27
  24.1 13.2 %all_gather.42 = f32[4,3,128]{2,1,0:T(4,128)S(1)} all-gather(f32[1,3,128]{2,1,0:T(4,128)S(1)} %select_n.435), channel_id=1, replica_groups=mesh['groups'=2,'age'=4,'span'=2,'blade'=2] {'age'}, dimensions={0}, use_global_device_ids=true | all-gather | bytes 7680 | tf_op jit(solution)/shard_map/all_gather | solution.py:16
  37.3 5.2 %all_gather.43 = f32[3,512]{1,0:T(4,128)S(1)} all-gather(f32[3,128]{1,0:T(4,128)S(1)} %reduce_sum.232), channel_id=1, replica_groups=mesh['groups'=2,'age'=4,'span'=2,'blade'=2] {'span','blade'}, dimensions={1}, use_global_device_ids=true | all-gather | bytes 7680 | tf_op jit(solution)/shard_map/all_gather | solution.py:161
  43.2 11.9 %all_gather.39 = f32[4,3,128]{2,1,0:T(4,128)S(1)} all-gather(f32[1,3,128]{2,1,0:T(4,128)S(1)} %select_n.419), channel_id=1, replica_groups=mesh['groups'=2,'age'=4,'span'=2,'blade'=2] {'age'}, dimensions={0}, use_global_device_ids=true | all-gather | bytes 7680 | tf_op jit(solution)/shard_map/all_gather | solution.py:16
  55.1 5.2 %all_gather.40 = f32[3,512]{1,0:T(4,128)S(1)} all-gather(f32[3,128]{1,0:T(4,128)S(1)} %reduce_sum.229), channel_id=1, replica_groups=mesh['groups'=2,'age'=4,'span'=2,'blade'=2] {'span','blade'}, dimensions={1}, use_global_device_ids=true | all-gather | bytes 7680 | tf_op jit(solution)/shard_map/all_gather | solution.py:161
  61.0 5.2 %all_gather.41 = f32[3,512]{1,0:T(4,128)S(1)} all-gather(f32[3,128]{1,0:T(4,128)S(1)} %div.142), channel_id=1, replica_groups=mesh['groups'=2,'age'=4,'span'=2,'blade'=2] {'span','blade'}, dimensions={1}, use_global_device_ids=true | all-gather | bytes 7680 | tf_op jit(solution)/shard_map/all_gather | solution.py:146
  66.6 9.9 %while.60 = (s32[]{:T(128)}, f32[16,1,3,128]{3,2,1,0:T(4,128)S(1)}, f32[3,512]{1,0:T(4,128)S(1)}, f32[16,1,3,128]{3,2,1,0:T(4,128)S(1)}, f32[3,512]{1,0:T(4,128)S(1)}, /*index=5*/s32[]{:T(128)}) while((s32[]{:T(128)}, f32[16,1,3,128]{3,2,1,0:T(4,128)S(1)}, f32[3,512]{1,0:T(4,128)S(1)}, f32[16,1,3,128]{3,2,1,0:T(4,128)S(1)}, ...), condition=%wide.region_10.11_spmd, body=%wide.region_6.10_spmd.sunk | while | flops 2293762 | bytes 2133581 | solution.py:101
  77.4 11.9 %all_gather.44 = f32[4,3,128]{2,1,0:T(4,128)S(1)} all-gather(f32[1,3,128]{2,1,0:T(4,128)S(1)} %select_n.443), channel_id=1, replica_groups=mesh['groups'=2,'age'=4,'span'=2,'blade'=2] {'age'}, dimensions={0}, use_global_device_ids=true | all-gather | bytes 7680 | tf_op jit(solution)/shard_map/all_gather | solution.py:16
  89.3 5.2 %all_gather.45 = f32[3,512]{1,0:T(4,128)S(1)} all-gather(f32[3,128]{1,0:T(4,128)S(1)} %reduce_sum.234), channel_id=1, replica_groups=mesh['groups'=2,'age'=4,'span'=2,'blade'=2] {'span','blade'}, dimensions={1}, use_global_device_ids=true | all-gather | bytes 7680 | tf_op jit(solution)/shard_map/all_gather | solution.py:161
  100.2 4.3 %collective-permute-done.3 = f32[4,2,18,1]{3,1,2,0:T(2,128)S(1)} collective-permute-done((f32[4,2,18,1]{3,1,2,0:T(2,128)S(1)}, f32[4,2,18,1]{3,1,2,0:T(2,128)S(1)}, u32[]{:S(2)}, u32[]{:S(2)}) %collective-permute-start.3) | collective-permute-done | bytes 608 | tf_op jit(solution)/shard_map/ppermute | solution.py:29
  108.9 4.3 %collective-permute-done.5 = f32[2,1,1,8,6,128]{5,3,0,4,2,1:T(8,128)S(1)} collective-permute-done((f32[2,1,1,8,6,128]{5,3,0,4,2,1:T(8,128)S(1)}, f32[2,1,1,8,6,128]{5,3,0,4,2,1:T(8,128)S(1)}, u32[]{:S(2)}, u32[]{:S(2)}) %collective-permute-start.5) | collective-permute-done | bytes 49184 | tf_op jit(solution)/shard_map/ppermute | solution.py:29
  117.5 4.4 %collective-permute-done.7 = f32[2,3,1,8,6,128]{5,3,0,4,2,1:T(8,128)S(1)} collective-permute-done((f32[2,3,1,8,6,128]{5,3,0,4,2,1:T(8,128)S(1)}, f32[2,3,1,8,6,128]{5,3,0,4,2,1:T(8,128)S(1)}, u32[]{:S(2)}, u32[]{:S(2)}) %collective-permute-start.7) | collective-permute-done | bytes 147488 | tf_op jit(solution)/shard_map/ppermute | solution.py:29
  123.4 19.9 %while.61 = (s32[]{:T(128)}, f32[16,1,3,128]{3,2,1,0:T(4,128)S(1)}, f32[16,1,3,1024]{3,0,2,1:T(8,128)S(1)}, f32[16,1,3,128]{3,2,1,0:T(4,128)S(1)}, f32[16,1,3,1024]{3,0,2,1:T(8,128)S(1)}, /*index=5*/s32[]{:T(128)}) while((s32[]{:T(128)}, f32[16,1,3,128]{3,2,1,0:T(4,128)S(1)}, f32[16,1,3,1024]{3,0,2,1:T(8,128)S(1)}, ...), condition=%wide.region_14.15_spmd, body=%wide.region_11.14_spmd.sunk | while | flops 4587522 | bytes 8560209 | solution.py:101
  147.5 7.5 %all-gather.2 = f32[4,1,128]{2,1,0:T(1,128)S(1)} all-gather(f32[1,1,128]{2,1,0:T(1,128)S(1)} %reshape.1387), channel_id=1, replica_groups=mesh['groups'=2,'age'=4,'span'=2,'blade'=2] {'age'}, dimensions={0}, use_global_device_ids=true | all-gather | bytes 2560 | tf_op jit(solution)/shard_map/all_gather | solution.py:16
  168.2 4.3 %collective-permute-done.12 = f32[4,2,18,1]{3,1,0,2:T(2,128)S(1)} collective-permute-done((f32[4,2,18,1]{3,1,0,2:T(2,128)S(1)}, f32[4,2,18,1]{3,1,0,2:T(2,128)S(1)}, u32[]{:S(2)}, u32[]{:S(2)}) %collective-permute-start.12) | collective-permute-done | bytes 608 | tf_op jit(solution)/shard_map/ppermute | solution.py:29
  177.6 4.3 %collective-permute-done.14 = f32[2,1,1,8,6,128]{5,3,0,4,2,1:T(8,128)S(1)} collective-permute-done((f32[2,1,1,8,6,128]{5,3,0,4,2,1:T(8,128)S(1)}, f32[2,1,1,8,6,128]{5,3,0,4,2,1:T(8,128)S(1)}, u32[]{:S(2)}, u32[]{:S(2)}) %collective-permute-start.14) | collective-permute-done | bytes 49184 | tf_op jit(solution)/shard_map/ppermute | solution.py:29
  184.9 9.9 %while.62 = (s32[]{:T(128)}, f32[16,1,3,128]{3,2,1,0:T(4,128)S(1)}, f32[3,512]{1,0:T(4,128)S(1)}, f32[16,1,3,128]{3,2,1,0:T(4,128)S(1)}, f32[3,512]{1,0:T(4,128)S(1)}, /*index=5*/s32[]{:T(128)}) while((s32[]{:T(128)}, f32[16,1,3,128]{3,2,1,0:T(4,128)S(1)}, f32[3,512]{1,0:T(4,128)S(1)}, f32[16,1,3,128]{3,2,1,0:T(4,128)S(1)}, ...), condition=%wide.region_21.22_spmd, body=%wide.region_17.21_spmd.sunk | while | flops 2293762 | bytes 2133581 | solution.py:101
  196.4 19.9 %while.63 = (s32[]{:T(128)}, f32[16,1,3,128]{3,2,1,0:T(4,128)S(1)}, f32[16,1,3,1024]{3,0,2,1:T(8,128)S(1)}, f32[16,1,3,128]{3,2,1,0:T(4,128)S(1)}, f32[16,1,3,1024]{3,0,2,1:T(8,128)S(1)}, /*index=5*/s32[]{:T(128)}) while((s32[]{:T(128)}, f32[16,1,3,128]{3,2,1,0:T(4,128)S(1)}, f32[16,1,3,1024]{3,0,2,1:T(8,128)S(1)}, ...), condition=%wide.region_25.26_spmd, body=%wide.region_22.25_spmd.sunk | while | flops 4587522 | bytes 8560209 | solution.py:101
  219.8 7.5 %all-gather.1 = f32[4,1,128]{2,1,0:T(1,128)S(1)} all-gather(f32[1,1,128]{2,1,0:T(1,128)S(1)} %reshape.1385), channel_id=1, replica_groups=mesh['groups'=2,'age'=4,'span'=2,'blade'=2] {'age'}, dimensions={0}, use_global_device_ids=true | all-gather | bytes 2560 | tf_op jit(solution)/shard_map/all_gather | solution.py:16
  237.0 4.6 %collective-permute-start.20 = (f32[4,2,18,1]{3,1,2,0:T(2,128)S(1)}, f32[4,2,18,1]{3,1,2,0:T(2,128)S(1)}, u32[]{:S(2)}, u32[]{:S(2)}) collective-permute-start(f32[4,2,18,1]{3,1,2,0:T(2,128)S(1)} %get-tuple-element.415), channel_id=1, source_target_pairs={{0,2},{1,3},{4,6},{5,7},{8,10},{9,11},{12,14},{13,15},{16,18},{17,... | collective-permute-start | bytes 1736 | tf_op jit(solution)/shard_map/ppermute | solution.py:27
  243.6 4.3 %collective-permute-done.21 = f32[4,2,18,1]{3,1,2,0:T(2,128)S(1)} collective-permute-done((f32[4,2,18,1]{3,1,2,0:T(2,128)S(1)}, f32[4,2,18,1]{3,1,2,0:T(2,128)S(1)}, u32[]{:S(2)}, u32[]{:S(2)}) %collective-permute-start.21) | collective-permute-done | bytes 608 | tf_op jit(solution)/shard_map/ppermute | solution.py:29
  252.6 10.1 %all-gather = f32[4,1,128]{2,1,0:T(1,128)S(1)} all-gather(f32[1,1,128]{2,1,0:T(1,128)S(1)} %reshape.1383), channel_id=1, replica_groups=mesh['groups'=2,'age'=4,'span'=2,'blade'=2] {'age'}, dimensions={0}, use_global_device_ids=true | all-gather | bytes 2560 | tf_op jit(solution)/shard_map/all_gather | solution.py:16
  265.9 9.9 %while.64 = (s32[]{:T(128)}, f32[16,1,3,128]{3,2,1,0:T(4,128)S(1)}, f32[3,512]{1,0:T(4,128)S(1)}, f32[16,1,3,128]{3,2,1,0:T(4,128)S(1)}, f32[3,512]{1,0:T(4,128)S(1)}, /*index=5*/s32[]{:T(128)}) while((s32[]{:T(128)}, f32[16,1,3,128]{3,2,1,0:T(4,128)S(1)}, f32[3,512]{1,0:T(4,128)S(1)}, f32[16,1,3,128]{3,2,1,0:T(4,128)S(1)}, ...), condition=%wide.region_32.33_spmd, body=%wide.region_28.32_spmd.sunk | while | flops 2293762 | bytes 2133581 | solution.py:101
  277.4 19.9 %while.65 = (s32[]{:T(128)}, f32[16,1,3,128]{3,2,1,0:T(4,128)S(1)}, f32[16,1,3,1024]{3,0,2,1:T(8,128)S(1)}, f32[16,1,3,128]{3,2,1,0:T(4,128)S(1)}, f32[16,1,3,1024]{3,0,2,1:T(8,128)S(1)}, /*index=5*/s32[]{:T(128)}) while((s32[]{:T(128)}, f32[16,1,3,128]{3,2,1,0:T(4,128)S(1)}, f32[16,1,3,1024]{3,0,2,1:T(8,128)S(1)}, ...), condition=%wide.region_36.37_spmd, body=%wide.region_33.36_spmd.sunk | while | flops 4587522 | bytes 8560209 | solution.py:101
  (1001 shorter events, 166.3 us)
Async XLA Ops:
  2.7 91.8 %collective-permute-start = (f32[4,2,1,64]{3,1,2,0:T(2,128)S(1)}, f32[4,2,1,64]{3,1,2,0:T(2,128)S(1)}, u32[]{:S(2)}, u32[]{:S(2)}) collective-permute-start(f32[4,2,1,64]{3,1,2,0:T(2,128)S(1)} %copy.362), channel_id=1, source_target_pairs={{0,4},{4,8},{8,12},{1,5},{5,9},{9,13},{2,6},{6,10},{10,14},{3,7},{... | collective-permute-start | bytes 6152 | tf_op jit(solution)/shard_map/ppermute | solution.py:27
  7.7 87.0 %collective-permute-start.1 = (f32[4,2,1,64]{3,1,2,0:T(2,128)S(1)}, f32[4,2,1,64]{3,1,2,0:T(2,128)S(1)}, u32[]{:S(2)}, u32[]{:S(2)}) collective-permute-start(f32[4,2,1,64]{3,1,2,0:T(2,128)S(1)} %copy.363), channel_id=1, source_target_pairs={{4,0},{8,4},{12,8},{5,1},{9,5},{13,9},{6,2},{10,6},{14,10},{7,3},{... | collective-permute-start | bytes 6152 | tf_op jit(solution)/shard_map/ppermute | solution.py:29
  94.8 5.4 %collective-permute-start.2 = (f32[4,2,18,1]{3,1,2,0:T(2,128)S(1)}, f32[4,2,18,1]{3,1,2,0:T(2,128)S(1)}, u32[]{:S(2)}, u32[]{:S(2)}) collective-permute-start(f32[4,2,18,1]{3,1,2,0:T(2,128)S(1)} %get-tuple-element.419), channel_id=1, source_target_pairs={{0,2},{1,3},{4,6},{5,7},{8,10},{9,11},{12,14},{13,15},{16,18},{17,... | collective-permute-start | bytes 1736 | tf_op jit(solution)/shard_map/ppermute | solution.py:27
  98.2 6.2 %collective-permute-start.3 = (f32[4,2,18,1]{3,1,2,0:T(2,128)S(1)}, f32[4,2,18,1]{3,1,2,0:T(2,128)S(1)}, u32[]{:S(2)}, u32[]{:S(2)}) collective-permute-start(f32[4,2,18,1]{3,1,2,0:T(2,128)S(1)} %get-tuple-element.420), channel_id=1, source_target_pairs={{2,0},{3,1},{6,4},{7,5},{10,8},{11,9},{14,12},{15,13},{18,16},{19,... | collective-permute-start | bytes 1736 | tf_op jit(solution)/shard_map/ppermute | solution.py:29
  107.2 6.1 %collective-permute-start.5 = (f32[2,1,1,8,6,128]{5,3,0,4,2,1:T(8,128)S(1)}, f32[2,1,1,8,6,128]{5,3,0,4,2,1:T(8,128)S(1)}, u32[]{:S(2)}, u32[]{:S(2)}) collective-permute-start(f32[2,1,1,8,6,128]{5,3,0,4,2,1:T(8,128)S(1)} %maximum_bitcast_fusion.3), channel_id=1, source_target_pairs={{4,0},{8,4},{12,8},{5,1},{9,5},{13,9},{6,2},{10,6},{14,10},{7,3},{... | collective-permute-start | bytes 147464 | tf_op jit(solution)/shard_map/ppermute | solution.py:29
  113.2 4.2 %collective-permute-start.6 = (f32[2,3,1,8,6,128]{5,3,0,4,2,1:T(8,128)S(1)}, f32[2,3,1,8,6,128]{5,3,0,4,2,1:T(8,128)S(1)}, u32[]{:S(2)}, u32[]{:S(2)}) collective-permute-start(f32[2,3,1,8,6,128]{5,3,0,4,2,1:T(8,128)S(1)} %pad_maximum_fusion.3), channel_id=1, source_target_pairs={{0,2},{1,3},{4,6},{5,7},{8,10},{9,11},{12,14},{13,15},{16,18},{17,... | collective-permute-start | bytes 442376 | tf_op jit(solution)/shard_map/ppermute | solution.py:27
  114.8 7.0 %collective-permute-start.7 = (f32[2,3,1,8,6,128]{5,3,0,4,2,1:T(8,128)S(1)}, f32[2,3,1,8,6,128]{5,3,0,4,2,1:T(8,128)S(1)}, u32[]{:S(2)}, u32[]{:S(2)}) collective-permute-start(f32[2,3,1,8,6,128]{5,3,0,4,2,1:T(8,128)S(1)} %pad_maximum_fusion.3), channel_id=1, source_target_pairs={{2,0},{3,1},{6,4},{7,5},{10,8},{11,9},{14,12},{15,13},{18,16},{19,... | collective-permute-start | bytes 442376 | tf_op jit(solution)/shard_map/ppermute | solution.py:29
  143.5 15.6 %collective-permute-start.8 = (f32[4,2,64]{2,1,0:T(2,128)S(1)}, f32[4,2,64]{2,1,0:T(2,128)S(1)}, u32[]{:S(2)}, u32[]{:S(2)}) collective-permute-start(f32[4,2,64]{2,1,0:T(2,128)S(1)} %get-tuple-element.424), channel_id=1, source_target_pairs={{0,4},{4,8},{8,12},{1,5},{5,9},{9,13},{2,6},{6,10},{10,14},{3,7},{... | collective-permute-start | bytes 6152 | tf_op jit(solution)/shard_map/ppermute | solution.py:39
  155.1 5.3 %collective-permute-start.9 = (f32[4,2,1,64]{3,1,0,2:T(2,128)S(1)}, f32[4,2,1,64]{3,1,0,2:T(2,128)S(1)}, u32[]{:S(2)}, u32[]{:S(2)}) collective-permute-start(f32[4,2,1,64]{3,1,0,2:T(2,128)S(1)} %get-tuple-element.423), channel_id=1, source_target_pairs={{0,4},{4,8},{8,12},{1,5},{5,9},{9,13},{2,6},{6,10},{10,14},{3,7},{... | collective-permute-start | bytes 6152 | tf_op jit(solution)/shard_map/ppermute | solution.py:27
  159.1 5.5 %collective-permute-start.10 = (f32[4,2,1,64]{3,1,0,2:T(2,128)S(1)}, f32[4,2,1,64]{3,1,0,2:T(2,128)S(1)}, u32[]{:S(2)}, u32[]{:S(2)}) collective-permute-start(f32[4,2,1,64]{3,1,0,2:T(2,128)S(1)} %fusion.57), channel_id=1, source_target_pairs={{4,0},{8,4},{12,8},{5,1},{9,5},{13,9},{6,2},{10,6},{14,10},{7,3},{... | collective-permute-start | bytes 6152 | tf_op jit(solution)/shard_map/ppermute | solution.py:29
  166.2 6.2 %collective-permute-start.12 = (f32[4,2,18,1]{3,1,0,2:T(2,128)S(1)}, f32[4,2,18,1]{3,1,0,2:T(2,128)S(1)}, u32[]{:S(2)}, u32[]{:S(2)}) collective-permute-start(f32[4,2,18,1]{3,1,0,2:T(2,128)S(1)} %get-tuple-element.418), channel_id=1, source_target_pairs={{2,0},{3,1},{6,4},{7,5},{10,8},{11,9},{14,12},{15,13},{18,16},{19,... | collective-permute-start | bytes 1736 | tf_op jit(solution)/shard_map/ppermute | solution.py:29
  174.0 3.7 %collective-permute-start.13 = (f32[2,1,1,8,6,128]{5,3,0,4,2,1:T(8,128)S(1)}, f32[2,1,1,8,6,128]{5,3,0,4,2,1:T(8,128)S(1)}, u32[]{:S(2)}, u32[]{:S(2)}) collective-permute-start(f32[2,1,1,8,6,128]{5,3,0,4,2,1:T(8,128)S(1)} %maximum_bitcast_fusion.4), channel_id=1, source_target_pairs={{0,4},{4,8},{8,12},{1,5},{5,9},{9,13},{2,6},{6,10},{10,14},{3,7},{... | collective-permute-start | bytes 147464 | tf_op jit(solution)/shard_map/ppermute | solution.py:27
  175.9 6.0 %collective-permute-start.14 = (f32[2,1,1,8,6,128]{5,3,0,4,2,1:T(8,128)S(1)}, f32[2,1,1,8,6,128]{5,3,0,4,2,1:T(8,128)S(1)}, u32[]{:S(2)}, u32[]{:S(2)}) collective-permute-start(f32[2,1,1,8,6,128]{5,3,0,4,2,1:T(8,128)S(1)} %maximum_bitcast_fusion.4), channel_id=1, source_target_pairs={{4,0},{8,4},{12,8},{5,1},{9,5},{13,9},{6,2},{10,6},{14,10},{7,3},{... | collective-permute-start | bytes 147464 | tf_op jit(solution)/shard_map/ppermute | solution.py:29
  181.9 13.1 %collective-permute-start.15 = (f32[2,3,1,8,6,128]{5,3,0,4,2,1:T(8,128)S(1)}, f32[2,3,1,8,6,128]{5,3,0,4,2,1:T(8,128)S(1)}, u32[]{:S(2)}, u32[]{:S(2)}) collective-permute-start(f32[2,3,1,8,6,128]{5,3,0,4,2,1:T(8,128)S(1)} %pad_maximum_fusion.4), channel_id=1, source_target_pairs={{0,2},{1,3},{4,6},{5,7},{8,10},{9,11},{12,14},{13,15},{16,18},{17,... | collective-permute-start | bytes 442376 | tf_op jit(solution)/shard_map/ppermute | solution.py:27
  183.5 11.5 %collective-permute-start.16 = (f32[2,3,1,8,6,128]{5,3,0,4,2,1:T(8,128)S(1)}, f32[2,3,1,8,6,128]{5,3,0,4,2,1:T(8,128)S(1)}, u32[]{:S(2)}, u32[]{:S(2)}) collective-permute-start(f32[2,3,1,8,6,128]{5,3,0,4,2,1:T(8,128)S(1)} %pad_maximum_fusion.4), channel_id=1, source_target_pairs={{2,0},{3,1},{6,4},{7,5},{10,8},{11,9},{14,12},{15,13},{18,16},{19,... | collective-permute-start | bytes 442376 | tf_op jit(solution)/shard_map/ppermute | solution.py:29
  216.6 14.7 %collective-permute-start.17 = (f32[4,2,64]{2,1,0:T(2,128)S(1)}, f32[4,2,64]{2,1,0:T(2,128)S(1)}, u32[]{:S(2)}, u32[]{:S(2)}) collective-permute-start(f32[4,2,64]{2,1,0:T(2,128)S(1)} %get-tuple-element.422), channel_id=1, source_target_pairs={{0,4},{4,8},{8,12},{1,5},{5,9},{9,13},{2,6},{6,10},{10,14},{3,7},{... | collective-permute-start | bytes 6152 | tf_op jit(solution)/shard_map/ppermute | solution.py:39
  227.4 5.3 %collective-permute-start.18 = (f32[4,2,1,64]{3,1,0,2:T(2,128)S(1)}, f32[4,2,1,64]{3,1,0,2:T(2,128)S(1)}, u32[]{:S(2)}, u32[]{:S(2)}) collective-permute-start(f32[4,2,1,64]{3,1,0,2:T(2,128)S(1)} %get-tuple-element.421), channel_id=1, source_target_pairs={{0,4},{4,8},{8,12},{1,5},{5,9},{9,13},{2,6},{6,10},{10,14},{3,7},{... | collective-permute-start | bytes 6152 | tf_op jit(solution)/shard_map/ppermute | solution.py:27
  231.3 5.5 %collective-permute-start.19 = (f32[4,2,1,64]{3,1,2,0:T(2,128)S(1)}, f32[4,2,1,64]{3,1,2,0:T(2,128)S(1)}, u32[]{:S(2)}, u32[]{:S(2)}) collective-permute-start(f32[4,2,1,64]{3,1,2,0:T(2,128)S(1)} %fusion.92), channel_id=1, source_target_pairs={{4,0},{8,4},{12,8},{5,1},{9,5},{13,9},{6,2},{10,6},{14,10},{7,3},{... | collective-permute-start | bytes 6152 | tf_op jit(solution)/shard_map/ppermute | solution.py:29
  237.0 6.5 %collective-permute-start.20 = (f32[4,2,18,1]{3,1,2,0:T(2,128)S(1)}, f32[4,2,18,1]{3,1,2,0:T(2,128)S(1)}, u32[]{:S(2)}, u32[]{:S(2)}) collective-permute-start(f32[4,2,18,1]{3,1,2,0:T(2,128)S(1)} %get-tuple-element.415), channel_id=1, source_target_pairs={{0,2},{1,3},{4,6},{5,7},{8,10},{9,11},{12,14},{13,15},{16,18},{17,... | collective-permute-start | bytes 1736 | tf_op jit(solution)/shard_map/ppermute | solution.py:27
  241.6 6.2 %collective-permute-start.21 = (f32[4,2,18,1]{3,1,2,0:T(2,128)S(1)}, f32[4,2,18,1]{3,1,2,0:T(2,128)S(1)}, u32[]{:S(2)}, u32[]{:S(2)}) collective-permute-start(f32[4,2,18,1]{3,1,2,0:T(2,128)S(1)} %get-tuple-element.416), channel_id=1, source_target_pairs={{2,0},{3,1},{6,4},{7,5},{10,8},{11,9},{14,12},{15,13},{18,16},{19,... | collective-permute-start | bytes 1736 | tf_op jit(solution)/shard_map/ppermute | solution.py:29
  249.3 13.7 %collective-permute-start.22 = (f32[2,1,1,8,6,128]{5,3,0,4,2,1:T(8,128)S(1)}, f32[2,1,1,8,6,128]{5,3,0,4,2,1:T(8,128)S(1)}, u32[]{:S(2)}, u32[]{:S(2)}) collective-permute-start(f32[2,1,1,8,6,128]{5,3,0,4,2,1:T(8,128)S(1)} %maximum_bitcast_fusion.5), channel_id=1, source_target_pairs={{0,4},{4,8},{8,12},{1,5},{5,9},{9,13},{2,6},{6,10},{10,14},{3,7},{... | collective-permute-start | bytes 147464 | tf_op jit(solution)/shard_map/ppermute | solution.py:27
  251.2 11.8 %collective-permute-start.23 = (f32[2,1,1,8,6,128]{5,3,0,4,2,1:T(8,128)S(1)}, f32[2,1,1,8,6,128]{5,3,0,4,2,1:T(8,128)S(1)}, u32[]{:S(2)}, u32[]{:S(2)}) collective-permute-start(f32[2,1,1,8,6,128]{5,3,0,4,2,1:T(8,128)S(1)} %maximum_bitcast_fusion.5), channel_id=1, source_target_pairs={{4,0},{8,4},{12,8},{5,1},{9,5},{13,9},{6,2},{10,6},{14,10},{7,3},{... | collective-permute-start | bytes 147464 | tf_op jit(solution)/shard_map/ppermute | solution.py:29
  263.0 12.9 %collective-permute-start.24 = (f32[2,3,1,8,6,128]{5,3,0,4,2,1:T(8,128)S(1)}, f32[2,3,1,8,6,128]{5,3,0,4,2,1:T(8,128)S(1)}, u32[]{:S(2)}, u32[]{:S(2)}) collective-permute-start(f32[2,3,1,8,6,128]{5,3,0,4,2,1:T(8,128)S(1)} %pad_maximum_fusion.5), channel_id=1, source_target_pairs={{0,2},{1,3},{4,6},{5,7},{8,10},{9,11},{12,14},{13,15},{16,18},{17,... | collective-permute-start | bytes 442376 | tf_op jit(solution)/shard_map/ppermute | solution.py:27
  264.6 11.3 %collective-permute-start.25 = (f32[2,3,1,8,6,128]{5,3,0,4,2,1:T(8,128)S(1)}, f32[2,3,1,8,6,128]{5,3,0,4,2,1:T(8,128)S(1)}, u32[]{:S(2)}, u32[]{:S(2)}) collective-permute-start(f32[2,3,1,8,6,128]{5,3,0,4,2,1:T(8,128)S(1)} %pad_maximum_fusion.5), channel_id=1, source_target_pairs={{2,0},{3,1},{6,4},{7,5},{10,8},{11,9},{14,12},{15,13},{18,16},{19,... | collective-permute-start | bytes 442376 | tf_op jit(solution)/shard_map/ppermute | solution.py:29
  (7 other events, 84.8 us)
